TPU v7x, 256 devices: a whole 4x4x8 slice. The times are simulated.
256 devices in a mesh: seg: 8 (over y, core), tm: 32 (over x, z).
Axes of the slice: x: 4, y: 4, z: 8, core: 2. Of those that a mesh axis runs over, the one named last changes fastest.
Arguments:
- transition: bfloat16 [512, 512, 512], P(('seg', 'tm')), may hold values from -1 to 1
- obs_gain: bfloat16 [512, 512, 512], P(('seg', 'tm')), may hold values from -0.0625 to 0.0625
- observed: bfloat16 [512, 4, 512], P(('seg', 'tm')), may hold values from -6 to 6
- init_mean: float32 [4, 512], replicated, may hold values from -6 to 6
- init_factor: float32 [512, 512], P('tm'), may hold values from -6 to 6
Outputs:
- means: float32 [512, 4, 512], P(('seg', 'tm'))
- factor_ends: float32 [8, 512, 512], P('seg', 'tm')
All inputs are finite; a program needn't handle non-finite values.
Results may differ from a plain program's by a relative error of at most 0.0003.
Values sent between devices are 32-bit elements; how exact they have to be, the bound alone decides.
A program may use at most 128 MiB of HBM per device.

v0:
```python
import functools

import jax
import jax.numpy as jnp
from jax import lax
from jax.experimental import pallas as pl
from jax.experimental.pallas import tpu as pltpu
from jax.sharding import PartitionSpec as P

MESH = pl.DeviceIdType.MESH
F32, BF16 = jnp.float32, jnp.bfloat16
D = 512
HALF = D // 2
ROWS = 32
NC = D // ROWS
NX = HALF // ROWS
LAG = 4
PAD = 8

NN = (((1,), (0,)), ((), ()))
NT = (((1,), (1,)), ((), ()))
TN = (((0,), (0,)), ((), ()))
TT = (((0,), (1,)), ((), ()))


def dot(a, b, dims=NN):
    return lax.dot_general(a, b, dims, preferred_element_type=F32)


def split(a):
    hi = a.astype(BF16)
    return hi, (a - hi.astype(F32)).astype(BF16)


def mm3(a, hi, lo, dims=NN):
    ah, al = split(a)
    n = a.shape[0]
    both = dot(jnp.concatenate([ah, al], axis=0), hi, dims)
    return both[:n] + both[n:] + dot(ah, lo, dims)


def mm2(a, exact):
    ah, al = split(a)
    n = a.shape[0]
    both = dot(jnp.concatenate([ah, al], axis=0), exact)
    return both[:n] + both[n:]


def kernel(
    t_ref, g_ref, o_ref, m0_ref, f0_ref, means_ref, ends_ref,
    zout, zin, whi, wlo, drv, cin, ch, csend,
    sphi, splo, px, wxhi, wxlo, xin, ab, abhi, ablo, pfhi, pflo,
    cs, cx, cseg, cown, m_in, m_out, f_in, f_out, f_box, inhi, inlo, e_in, e_out, e_half, e_x, e_next,
    zs, zr, cs_s, cs_r, ch_s, ch_r, xs, xr, abx_s, abx_r, abz_s, abz_r,
    cx_s, cx_r, m_s, m_r, f0_s, f0_r, f_s, f_r, fb_s, fb_r, e_s, e_r, ex_s, ex_r,
):
    seg = lax.axis_index("seg")
    tm = lax.axis_index("tm")
    c = seg % 2
    x, z = tm // 8, tm % 8
    zh, zi = z // 4, z % 4
    row = zh == c
    pos = jnp.where(row, zi, 3 - zi)
    nz = jnp.where(row, (z + 1) % 8, (z + 7) % 8)
    end = pos == 3
    inner = (x == 1) | (x == 2)
    root = end & inner
    outer = end & jnp.logical_not(inner)
    first, last = seg == 0, seg == 7
    xroot = jnp.where(x < 2, 1, 2)
    xouter = jnp.where(x < 2, 0, 3)

    def end_z(core, half):
        return jnp.where(core == 0, 3 + half, 7 * half)

    def did(s, xx, zz):
        return (s, xx * 8 + zz)

    myend = end_z(c, zh)

    def rcopy(src, dst, ssem, rsem, dev):
        return pltpu.make_async_remote_copy(
            src_ref=src, dst_ref=dst, send_sem=ssem, recv_sem=rsem, device_id=dev, device_id_type=MESH
        )

    def got(dst, rsem):
        rcopy(dst, dst, rsem, rsem, did(seg, x, nz)).wait_recv()

    barrier = pltpu.get_barrier_semaphore()

    def greet(dev):
        pl.semaphore_signal(barrier, inc=1, device_id=dev, device_id_type=MESH)

    for k in range(1, 8):
        greet(did(seg, x, (z + k) % 8))
    for k in range(1, 4):
        greet(did(seg, (x + k) % 4, z))

    @pl.when(jnp.logical_not(inner))
    def _():
        greet(did(seg, xroot, myend))

    @pl.when(root)
    def _():
        for k in range(4):
            greet(did(seg, xouter, zh * 4 + k))

        @pl.when(jnp.logical_not(last))
        def _():
            greet(did(seg + 1, x, end_z(1 - c, zh)))

        @pl.when(jnp.logical_not(first))
        def _():
            greet(did(seg - 1, x, end_z(1 - c, zh)))

    @pl.when(root & (x == 1) & jnp.logical_not(last))
    def _():
        greet(did(seg + 1, 0, end_z(1 - c, zh)))

    @pl.when(end & (x == 0) & jnp.logical_not(first))
    def _():
        greet(did(seg - 1, 1, end_z(1 - c, zh)))

    one = lambda p: jnp.where(p, 1, 0)
    greets = (
        10 + one(jnp.logical_not(inner))
        + one(root) * (4 + one(jnp.logical_not(last)) + one(jnp.logical_not(first)))
        + one(root & (x == 1) & jnp.logical_not(last)) + one(end & (x == 0) & jnp.logical_not(first))
    )

    def put_map(m):
        @pl.when(pos == 0)
        def _():
            zout[...] = m

        @pl.when(pos > 0)
        def _():
            hi, lo = split(m)
            whi[...] = hi
            wlo[...] = lo

    @pl.when(row)
    def _():
        put_map(dot(t_ref[0], t_ref[1]))

    @pl.when(jnp.logical_not(row))
    def _():
        put_map(dot(t_ref[1], t_ref[0], TT))

    pad = jnp.zeros((PAD - 4, D), F32)
    for s in range(2):
        drv[s] = jnp.concatenate([dot(o_ref[s], g_ref[s]), pad], axis=0)

    @pl.when(zi == 0)
    def _():
        cin[...] = jnp.zeros_like(cin)

    pl.semaphore_wait(barrier, greets)

    block = jnp.where(x == xroot, 0, 4) + zi

    def f0_copy():
        return rcopy(f0_ref, f_in.at[block], f0_s, f0_r.at[block], did(seg, xroot, myend))

    @pl.when(first & jnp.logical_not(root))
    def _():
        f0_copy().start()

    @pl.when(first & root)
    def _():
        f_in[block] = f0_ref[...]

    def two_steps(m):
        m1 = mm2(m, t_ref[0]) + drv[0]
        return m1, mm2(m1, t_ref[1]) + drv[1]

    def c_next():
        return rcopy(csend, cin, cs_s, cs_r, did(seg, x, (z + 1) % 8))

    def c_end(half):
        return rcopy(csend, ch.at[zh], ch_s.at[half], ch_r.at[zh], did(seg, x, end_z(c, half)))

    def c_step():
        @pl.when(zi > 0)
        def _():
            got(cin, cs_r)

        csend[...] = two_steps(cin[...])[1]

        @pl.when(zi < 3)
        def _():
            c_next().start()

        @pl.when(zi == 3)
        def _():
            for half in range(2):
                away = end_z(c, half) != z

                @pl.when(away)
                def _():
                    c_end(half).start()

                @pl.when(jnp.logical_not(away))
                def _():
                    ch[zh] = csend[...]

    turn = jnp.where(row, 0, jnp.where(pos == 1, NC // 2, jnp.where(pos == 0, NC, 0)))
    slot = jnp.where(end, 1, 0)

    def piece(k):
        return pl.ds(pl.multiple_of(k * ROWS, ROWS), ROWS)

    def z_copy(k):
        return rcopy(
            zout.at[piece(k)], zin.at[slot, piece(k)], zs.at[k], zr.at[slot, k], did(seg, x, nz)
        )

    def z_body(k, _):
        pl.when(k == turn)(c_step)

        @pl.when(k < NC)
        def _():
            @pl.when(pos > 0)
            def _():
                got(zin.at[0, piece(k)], zr.at[0, k])
                zout[piece(k), :] = mm3(zin[0, piece(k), :], whi[...], wlo[...])

            z_copy(k).start()

        return 0

    lax.fori_loop(0, NC + 1, z_body, 0)

    @pl.when(row & (pos > 0))
    def _():
        hi, lo = split(zin[0])
        inhi[...] = hi
        inlo[...] = lo

    iv = jnp.where(x < 2, 1, 0)
    w = jnp.where(x == 1, 0, 1)

    def half_rows(k, half):
        return pl.ds(pl.multiple_of(half * HALF + k * ROWS, ROWS), ROWS)

    def x_copy(k):
        return rcopy(px.at[half_rows(k, zh)], xin.at[piece(k)], xs.at[k], xr.at[k], did(seg, xroot, z))

    def abx_copy(k):
        return rcopy(
            ab.at[w, half_rows(k, zh)], ab.at[w, half_rows(k, zh)], abx_s.at[k], abx_r.at[k], did(seg, 3 - x, z)
        )

    def abz_copy(k, which):
        return rcopy(
            ab.at[which, half_rows(k, zh)], ab.at[which, half_rows(k, zh)],
            abz_s.at[which, k], abz_r.at[which, k], did(seg, x, nz),
        )

    def cx_copy(which, send, to):
        return rcopy(cown, cs.at[which], cx_s.at[send], cx_r.at[which], did(seg, to, z))

    @pl.when(end)
    def _():
        def x_wait(k, _):
            got(zin.at[1, piece(k)], zr.at[1, k])
            return 0

        lax.fori_loop(0, NC, x_wait, 0)
        ia = jnp.where((zh == 0) == (x < 2), 0, 1)
        hi, lo = split(zout[...])
        sphi[ia] = hi
        splo[ia] = lo
        hi, lo = split(zin[1])
        sphi[1 - ia] = hi
        splo[1 - ia] = lo
        for core, dims in ((0, NT), (1, TN)):
            @pl.when(c == core)
            def _():
                p = dot(sphi[0], sphi[1], dims)
                p += dot(splo[0], sphi[1], dims)
                p += dot(sphi[0], splo[1], dims)
                px[...] = p

        @pl.when(outer)
        def _():
            for k in range(NX):
                x_copy(k).start()

        hi, lo = split(px[...])
        wxhi[...] = hi
        wxlo[...] = lo

        @pl.when(zh != c)
        def _():
            got(ch.at[zh], ch_r.at[zh])

        got(ch.at[1 - zh], ch_r.at[1 - zh])
        for core, dims in ((0, NT), (1, NN)):
            @pl.when(c == core)
            def _():
                cx[...] = mm3(ch[0], sphi[iv], splo[iv], dims) + ch[1]

        @pl.when(x == 0)
        def _():
            cown[...] = cx[...]
            cx_copy(0, 0, 1).start()

        @pl.when(x == 1)
        def _():
            got(cs.at[0], cx_r.at[0])
            cown[...] = mm3(cs[0], wxhi[...], wxlo[...]) + cx[...]
            cs[1] = cown[...]
            cx_copy(1, 0, 2).start()

        @pl.when(x == 2)
        def _():
            cown[...] = cx[...]
            cx_copy(2, 0, 3).start()

        @pl.when(x == 3)
        def _():
            got(cs.at[2], cx_r.at[2])
            cown[...] = mm3(cs[2], wxhi[...], wxlo[...], NT) + cx[...]
            cx_copy(3, 0, 2).start()
            cx_copy(3, 1, 1).start()

    @pl.when(root)
    def _():
        def x_body(k, _):
            @pl.when(k < NX)
            def _():
                got(xin.at[piece(k)], xr.at[k])
                ab[w, half_rows(k, zh), :] = mm3(xin[piece(k), :], wxhi[...], wxlo[...])
                abx_copy(k).start()
                abz_copy(k, w).start()

            @pl.when(k >= LAG)
            def _():
                got(ab.at[1 - w, half_rows(k - LAG, zh)], abx_r.at[k - LAG])
                abz_copy(k - LAG, 1 - w).start()

            return 0

        lax.fori_loop(0, NX + LAG, x_body, 0)

        def ab_wait(k, _):
            for which in range(2):
                got(ab.at[which, half_rows(k, 1 - zh)], abz_r.at[which, k])
            return 0

        lax.fori_loop(0, NX, ab_wait, 0)
        for which in range(2):
            hi, lo = split(ab[which])
            abhi[which] = hi
            ablo[which] = lo
        p = dot(abhi[0], abhi[1], NT)
        p += dot(ablo[0], abhi[1], NT)
        p += dot(abhi[0], ablo[1], NT)
        hi, lo = split(p)
        pfhi[...] = hi
        pflo[...] = lo

        @pl.when(x == 2)
        def _():
            got(cs.at[1], cx_r.at[1])

        got(cs.at[3], cx_r.at[3])
        cseg[...] = mm3(cs[1], abhi[1], ablo[1], NT) + cs[3]

    m0 = jnp.concatenate([m0_ref[...], pad], axis=0)
    chained = root | (end & (x == 0))

    @pl.when(chained & first)
    def _():
        m_in[...] = m0

    @pl.when(chained & jnp.logical_not(first))
    def _():
        got(m_in, m_r)

    def m_copy(to, send):
        return rcopy(m_out, m_in, m_s.at[send], m_r, did(seg + 1, to, end_z(1 - c, zh)))

    def f_copy(q):
        part = pl.ds(2 * q, 2)
        return rcopy(f_out.at[part], f_in.at[part], f_s.at[q], f_r.at[q], did(seg + 1, x, end_z(1 - c, zh)))

    def owner(blk):
        return jnp.where(blk < 4, x, xouter), zh * 4 + blk % 4

    def fb_copy(blk):
        ox, oz = owner(blk)
        return rcopy(f_out.at[blk], f_box, fb_s.at[blk], fb_r, did(seg, ox, oz))

    def ex_copy(to):
        return rcopy(e_out, e_x, ex_s, ex_r, did(seg, to, z))

    @pl.when(root)
    def _():
        @pl.when(jnp.logical_not(last))
        def _():
            m_out[...] = mm3(m_in[...], pfhi[...], pflo[...]) + cseg[...]
            m_copy(x, 0).start()

            @pl.when(x == 1)
            def _():
                m_copy(0, 1).start()

        @pl.when(x == 2)
        def _():
            e_x[...] = mm3(m_in[...], abhi[0], ablo[0]) + cs[1]
            e_out[...] = mm3(e_x[...], wxhi[...], wxlo[...], NT) + cx[...]
            ex_copy(3).start()

        def f_body(q, _):
            for u in range(2):
                blk = 2 * q + u

                @pl.when(first & (blk != block))
                def _():
                    got(f_in.at[blk], f0_r.at[blk])

            @pl.when(jnp.logical_not(first))
            def _():
                got(f_in.at[pl.ds(2 * q, 2)], f_r.at[q])

            rows = jnp.concatenate([f_in[2 * q], f_in[2 * q + 1]], axis=0)
            rows = mm3(rows, pfhi[...], pflo[...])
            f_out[2 * q] = rows[:16]
            f_out[2 * q + 1] = rows[16:]

            @pl.when(jnp.logical_not(last))
            def _():
                f_copy(q).start()

            for u in range(2):
                blk = 2 * q + u

                @pl.when(blk != block)
                def _():
                    fb_copy(blk).start()

                @pl.when(blk == block)
                def _():
                    ends_ref[0] = f_out[blk]

            return 0

        lax.fori_loop(0, 4, f_body, 0)

    @pl.when(end & (x == 0))
    def _():
        e_out[...] = mm3(m_in[...], wxhi[...], wxlo[...]) + cx[...]
        ex_copy(1).start()
        e_x[...] = m_in[...]

    @pl.when(end & ((x == 1) | (x == 3)))
    def _():
        got(e_x, ex_r)

    @pl.when(end & (zh == 0))
    def _():
        e_half[...] = e_x[...]

    for core, dims in ((0, NN), (1, NT)):
        @pl.when(end & (zh == 1) & (c == core))
        def _():
            e_half[...] = mm3(e_x[...], sphi[1 - iv], splo[1 - iv], dims) + ch[0]

    def e_copy(src, to, send):
        return rcopy(src, e_in, e_s.at[send], e_r, did(seg, x, to))

    @pl.when(end & row)
    def _():
        for k in range(3):
            e_copy(e_half, zh * 4 + k, k).start()

    @pl.when(jnp.logical_not(end))
    def _():
        got(e_in, e_r)
        e_half[...] = e_in[...]

    @pl.when(row & (pos > 0))
    def _():
        e_half_entry = mm3(e_half[...], inhi[...], inlo[...]) + cin[...]
        m1, m2 = two_steps(e_half_entry)
        means_ref[0] = m1[:4]
        means_ref[1] = m2[:4]

    @pl.when(jnp.logical_not(row & (pos > 0)))
    def _():
        m1, m2 = two_steps(e_half[...])

        @pl.when(jnp.logical_not(row) & (zi < 3))
        def _():
            e_next[...] = m2
            e_copy(e_next, z + 1, 0).start()

        means_ref[0] = m1[:4]
        means_ref[1] = m2[:4]

    @pl.when(jnp.logical_not(root))
    def _():
        got(f_box, fb_r)
        ends_ref[0] = f_box[...]

    def z_done(k, _):
        z_copy(k).wait_send()
        return 0

    lax.fori_loop(0, NC, z_done, 0)

    @pl.when(zi < 3)
    def _():
        c_next().wait_send()

    @pl.when(zi == 3)
    def _():
        for half in range(2):
            @pl.when(end_z(c, half) != z)
            def _():
                c_end(half).wait_send()

    @pl.when(first & jnp.logical_not(root))
    def _():
        f0_copy().wait_send()

    @pl.when(outer)
    def _():
        for k in range(NX):
            x_copy(k).wait_send()

        @pl.when(x == 0)
        def _():
            cx_copy(0, 0, 1).wait_send()

        @pl.when(x == 3)
        def _():
            cx_copy(3, 0, 2).wait_send()
            cx_copy(3, 1, 1).wait_send()

    @pl.when(root)
    def _():
        def ab_done(k, _):
            abx_copy(k).wait_send()
            for which in range(2):
                abz_copy(k, which).wait_send()
            return 0

        lax.fori_loop(0, NX, ab_done, 0)
        cx_copy(1, 0, 3).wait_send()

        @pl.when(jnp.logical_not(last))
        def _():
            m_copy(x, 0).wait_send()

            @pl.when(x == 1)
            def _():
                m_copy(0, 1).wait_send()

            for q in range(4):
                f_copy(q).wait_send()

        for blk in range(8):
            @pl.when(blk != block)
            def _():
                fb_copy(blk).wait_send()

    @pl.when(end & ((x == 0) | (x == 2)))
    def _():
        ex_copy(1).wait_send()

    @pl.when(end & row)
    def _():
        for k in range(3):
            e_copy(e_half, zh * 4 + k, k).wait_send()

    @pl.when(jnp.logical_not(row) & (zi < 3))
    def _():
        e_copy(e_next, z + 1, 0).wait_send()


def per_device(transition, obs_gain, observed, init_mean, init_factor):
    vm = pl.BlockSpec(memory_space=pltpu.VMEM)
    f, b = (lambda *s: pltpu.VMEM(s, F32)), (lambda *s: pltpu.VMEM(s, BF16))
    dma = lambda *s: pltpu.SemaphoreType.DMA(s) if s else pltpu.SemaphoreType.DMA
    scratch = [
        f(D, D), f(2, D, D), b(D, D), b(D, D), f(2, PAD, D), f(PAD, D), f(2, PAD, D), f(PAD, D),
        b(2, D, D), b(2, D, D), f(D, D), b(D, D), b(D, D), f(HALF, D), f(2, D, D), b(2, D, D), b(2, D, D), b(D, D), b(D, D),
        f(4, PAD, D), f(PAD, D), f(PAD, D), f(PAD, D), f(PAD, D), f(PAD, D), f(8, 16, D), f(8, 16, D), f(16, D), b(D, D), b(D, D),
        f(PAD, D), f(PAD, D), f(PAD, D), f(PAD, D), f(PAD, D),
        dma(NC), dma(2, NC), dma(), dma(), dma(2), dma(2), dma(NX), dma(NX), dma(NX), dma(NX), dma(2, NX), dma(2, NX),
        dma(2), dma(4), dma(2), dma(), dma(), dma(8), dma(4), dma(4), dma(8), dma(), dma(3), dma(), dma(), dma(),
    ]
    return pl.pallas_call(
        kernel,
        out_shape=(jax.ShapeDtypeStruct((2, 4, D), F32), jax.ShapeDtypeStruct((1, 16, D), F32)),
        in_specs=[vm] * 5,
        out_specs=(vm, vm),
        scratch_shapes=scratch,
        compiler_params=pltpu.CompilerParams(
            collective_id=0, has_side_effects=True, vmem_limit_bytes=56 * 2**20
        ),
        name="filter_flow",
    )(transition, obs_gain, observed, init_mean, init_factor)


def solution(mesh):
    placed = P(("seg", "tm"), None, None)
    return jax.shard_map(
        per_device,
        mesh=mesh,
        in_specs=(placed, placed, placed, P(), P("tm", None)),
        out_specs=(placed, P("seg", "tm", None)),
        check_vma=False,
    )
```

profile of v0, /device:TPU:123, one launch (start us, length us, event | category | flops | bytes accessed | tf_op | source)
XLA Modules:
  0.0 102.5 jit_solution(2595197650859240103)
XLA Ops:
  0.6 99.9 %filter_flow.1 = (f32[2,4,512]{2,1,0:T(4,128)}, f32[1,16,512]{2,1,0:T(8,128)}) custom-call(bf16[2,512,512]{2,1,0:T(8,128)(2,1)} %t_ref.1, bf16[2,512,512]{2,1,0:T(8,128)(2,1)} %g_ref.1, bf16[2,4,512]{2,1,0:T(4,128)(2,1)} %o_ref.1, f32[4,512]{1,0:T(4,128)} %m0_ref.1, f32[16,512]{1,0:T(8,128)} %f0_ref.1), custom_call_target="tpu_custom_call" | custom-call | tf_op jit(solution)/shard_map/filter_flow/pallas_call | solution.py:596
  100.5 0.0 copy-start
  100.6 1.3 %copy.9 = f32[2,4,512]{2,1,0:T(4,128)} copy(f32[2,4,512]{2,1,0:T(4,128)} %get-tuple-element.4) | data formatting | bytes 32768
  101.9 0.0 copy-done
  101.9 0.6 copy.10
Async XLA Ops:
  100.5 1.3 %copy-start = (f32[1,16,512]{2,1,0:T(8,128)S(1)}, f32[1,16,512]{2,1,0:T(8,128)}, u32[]{:S(2)}) copy-start(f32[1,16,512]{2,1,0:T(8,128)} %get-tuple-element.5) | copy-start | bytes 98308
where the time goes:
time: 103 us
  Pallas kernels  99.9 us (97%)
  local copies, waits for them, and re-layouts  1.95 us (2%)
    pallas_call x1, Pallas kernels, per_device(): pl.pallas_call(kernel, out_shape=(jax.ShapeDtypeStruct((2, 4, D), F32), j...  99.9 us

commit v1 on v0

--- a/solution.py
+++ b/solution.py
@@ -50,13 +50,17 @@
     t_ref, g_ref, o_ref, m0_ref, f0_ref, means_ref, ends_ref,
     zout, zin, whi, wlo, drv, cin, ch, csend,
     sphi, splo, px, wxhi, wxlo, xin, ab, abhi, ablo, pfhi, pflo,
-    cs, cx, cseg, cown, m_in, m_out, f_in, f_out, f_box, inhi, inlo, e_in, e_out, e_half, e_x, e_next,
-    zs, zr, cs_s, cs_r, ch_s, ch_r, xs, xr, abx_s, abx_r, abz_s, abz_r,
+    cs, cx, cseg, cown, m_in, m_out, f_in, f_out, inhi, inlo, e_in, e_out, e_half, e_x, e_next,
+    zs, zr, cs_s, cs_r, ch_s, ch_r, xs, xr, abx_s, abx_r, abm_s, abm_r, abz_s, abz_r,
     cx_s, cx_r, m_s, m_r, f0_s, f0_r, f_s, f_r, fb_s, fb_r, e_s, e_r, ex_s, ex_r,
 ):
     seg = lax.axis_index("seg")
     tm = lax.axis_index("tm")
-    c = seg % 2
+
+    def way(s):
+        return (s + s // 2) % 2
+
+    c = way(seg)
     x, z = tm // 8, tm % 8
     zh, zi = z // 4, z % 4
     row = zh == c
@@ -91,10 +95,38 @@
     def greet(dev):
         pl.semaphore_signal(barrier, inc=1, device_id=dev, device_id_type=MESH)
 
-    for k in range(1, 8):
-        greet(did(seg, x, (z + k) % 8))
-    for k in range(1, 4):
-        greet(did(seg, (x + k) % 4, z))
+    pz = jnp.where(row, z - 1, z + 1)
+
+    @pl.when(pos < 3)
+    def _():
+        greet(did(seg, x, myend))
+
+    @pl.when((pos < 2) | end)
+    def _():
+        greet(did(seg, x, nz))
+
+    @pl.when((pos == 1) | (pos == 2))
+    def _():
+        greet(did(seg, x, pz))
+
+    @pl.when((pos == 0) & jnp.logical_not(row))
+    def _():
+        greet(did(seg, x, end_z(c, 1 - zh)))
+
+    @pl.when(end)
+    def _():
+        for k in range(1, 4):
+            greet(did(seg, x, zh * 4 + (zi + k) % 4))
+
+        @pl.when(row)
+        def _():
+            greet(did(seg, x, (1 - zh) * 4 + 3))
+
+    for here, others in ((0, (1,)), (1, (0, 2, 3)), (2, (1, 3)), (3, (2, 1))):
+        @pl.when(end & (x == here))
+        def _():
+            for k in others:
+                greet(did(seg, k, z))
 
     @pl.when(jnp.logical_not(inner))
     def _():
@@ -107,23 +139,24 @@
 
         @pl.when(jnp.logical_not(last))
         def _():
-            greet(did(seg + 1, x, end_z(1 - c, zh)))
+            greet(did(seg + 1, x, end_z(way(seg + 1), zh)))
 
         @pl.when(jnp.logical_not(first))
         def _():
-            greet(did(seg - 1, x, end_z(1 - c, zh)))
+            greet(did(seg - 1, x, end_z(way(seg - 1), zh)))
 
     @pl.when(root & (x == 1) & jnp.logical_not(last))
     def _():
-        greet(did(seg + 1, 0, end_z(1 - c, zh)))
+        greet(did(seg + 1, 0, end_z(way(seg + 1), zh)))
 
     @pl.when(end & (x == 0) & jnp.logical_not(first))
     def _():
-        greet(did(seg - 1, 1, end_z(1 - c, zh)))
+        greet(did(seg - 1, 1, end_z(way(seg - 1), zh)))
 
     one = lambda p: jnp.where(p, 1, 0)
     greets = (
-        10 + one(jnp.logical_not(inner))
+        one(pos < 3) + one((pos < 2) | end) + one((pos == 1) | (pos == 2)) + one((pos == 0) & jnp.logical_not(row))
+        + one(end) * (3 + one(row) + jnp.where(x == 0, 1, jnp.where(x == 1, 3, 2))) + one(jnp.logical_not(inner))
         + one(root) * (4 + one(jnp.logical_not(last)) + one(jnp.logical_not(first)))
         + one(root & (x == 1) & jnp.logical_not(last)) + one(end & (x == 0) & jnp.logical_not(first))
     )
@@ -156,19 +189,6 @@
         cin[...] = jnp.zeros_like(cin)
 
     pl.semaphore_wait(barrier, greets)
-
-    block = jnp.where(x == xroot, 0, 4) + zi
-
-    def f0_copy():
-        return rcopy(f0_ref, f_in.at[block], f0_s, f0_r.at[block], did(seg, xroot, myend))
-
-    @pl.when(first & jnp.logical_not(root))
-    def _():
-        f0_copy().start()
-
-    @pl.when(first & root)
-    def _():
-        f_in[block] = f0_ref[...]
 
     def two_steps(m):
         m1 = mm2(m, t_ref[0]) + drv[0]
@@ -215,6 +235,8 @@
             zout.at[piece(k)], zin.at[slot, piece(k)], zs.at[k], zr.at[slot, k], did(seg, x, nz)
         )
 
+    ia = jnp.where((zh == 0) == (x < 2), 0, 1)
+
     def z_body(k, _):
         pl.when(k == turn)(c_step)
 
@@ -223,13 +245,37 @@
             @pl.when(pos > 0)
             def _():
                 got(zin.at[0, piece(k)], zr.at[0, k])
-                zout[piece(k), :] = mm3(zin[0, piece(k), :], whi[...], wlo[...])
+                v = mm3(zin[0, piece(k), :], whi[...], wlo[...])
+                zout[piece(k), :] = v
+
+                @pl.when(end)
+                def _():
+                    sphi[ia, piece(k), :], splo[ia, piece(k), :] = split(v)
+
 
             z_copy(k).start()
 
         return 0
 
     lax.fori_loop(0, NC + 1, z_body, 0)
+
+    def z_sent():
+        def z_done(k, _):
+            z_copy(k).wait_send()
+            return 0
+
+        lax.fori_loop(0, NC, z_done, 0)
+
+        @pl.when(zi < 3)
+        def _():
+            c_next().wait_send()
+
+        @pl.when(zi == 3)
+        def _():
+            for half in range(2):
+                @pl.when(end_z(c, half) != z)
+                def _():
+                    c_end(half).wait_send()
 
     @pl.when(row & (pos > 0))
     def _():
@@ -257,6 +303,14 @@
             abz_s.at[which, k], abz_r.at[which, k], did(seg, x, nz),
         )
 
+    def abx_more(k):
+        return rcopy(
+            ab.at[w, half_rows(k, 1 - zh)], ab.at[w, half_rows(k, 1 - zh)], abm_s.at[k], abm_r.at[k], did(seg, 3 - x, z)
+        )
+
+    def ab_split(which, rows):
+        abhi[which, rows, :], ablo[which, rows, :] = split(ab[which, rows, :])
+
     def cx_copy(which, send, to):
         return rcopy(cown, cs.at[which], cx_s.at[send], cx_r.at[which], did(seg, to, z))
 
@@ -264,28 +318,26 @@
     def _():
         def x_wait(k, _):
             got(zin.at[1, piece(k)], zr.at[1, k])
+            sphi[1 - ia, piece(k), :], splo[1 - ia, piece(k), :] = split(zin[1, piece(k), :])
             return 0
 
         lax.fori_loop(0, NC, x_wait, 0)
-        ia = jnp.where((zh == 0) == (x < 2), 0, 1)
-        hi, lo = split(zout[...])
-        sphi[ia] = hi
-        splo[ia] = lo
-        hi, lo = split(zin[1])
-        sphi[1 - ia] = hi
-        splo[1 - ia] = lo
-        for core, dims in ((0, NT), (1, TN)):
-            @pl.when(c == core)
-            def _():
-                p = dot(sphi[0], sphi[1], dims)
-                p += dot(splo[0], sphi[1], dims)
-                p += dot(sphi[0], splo[1], dims)
-                px[...] = p
-
-        @pl.when(outer)
-        def _():
-            for k in range(NX):
-                x_copy(k).start()
+        for half in (zh, 1 - zh):
+            part = pl.ds(pl.multiple_of(half * HALF, HALF), HALF)
+            for core, dims in ((0, NT), (1, TN)):
+                @pl.when(c == core)
+                def _():
+                    at = (part, slice(None)) if core == 0 else (slice(None), part)
+                    p = dot(sphi[(0, *at)], sphi[1], dims)
+                    p += dot(splo[(0, *at)], sphi[1], dims)
+                    p += dot(sphi[(0, *at)], splo[1], dims)
+                    px[part, :] = p
+
+            if half is zh:
+                @pl.when(outer)
+                def _():
+                    for k in range(NX):
+                        x_copy(k).start()
 
         hi, lo = split(px[...])
         wxhi[...] = hi
@@ -331,29 +383,48 @@
             @pl.when(k < NX)
             def _():
                 got(xin.at[piece(k)], xr.at[k])
-                ab[w, half_rows(k, zh), :] = mm3(xin[piece(k), :], wxhi[...], wxlo[...])
+                v = mm3(xin[piece(k), :], wxhi[...], wxlo[...])
+                mine = half_rows(k, zh)
+                ab[w, mine, :] = v
                 abx_copy(k).start()
                 abz_copy(k, w).start()
+                abhi[w, mine, :], ablo[w, mine, :] = split(v)
 
             @pl.when(k >= LAG)
             def _():
-                got(ab.at[1 - w, half_rows(k - LAG, zh)], abx_r.at[k - LAG])
-                abz_copy(k - LAG, 1 - w).start()
+                j = k - LAG
+                got(ab.at[1 - w, half_rows(j, zh)], abx_r.at[j])
+
+                @pl.when(j % 2 == 0)
+                def _():
+                    abz_copy(j, 1 - w).start()
+
+                ab_split(1 - w, half_rows(j, zh))
+                got(ab.at[w, half_rows(j, 1 - zh)], abz_r.at[w, j])
+
+                @pl.when(j % 2 == 1)
+                def _():
+                    abx_more(j).start()
+
+                ab_split(w, half_rows(j, 1 - zh))
 
             return 0
 
         lax.fori_loop(0, NX + LAG, x_body, 0)
 
         def ab_wait(k, _):
-            for which in range(2):
-                got(ab.at[which, half_rows(k, 1 - zh)], abz_r.at[which, k])
+            @pl.when(k % 2 == 0)
+            def _():
+                got(ab.at[1 - w, half_rows(k, 1 - zh)], abz_r.at[1 - w, k])
+
+            @pl.when(k % 2 == 1)
+            def _():
+                got(ab.at[1 - w, half_rows(k, 1 - zh)], abm_r.at[k])
+
+            ab_split(1 - w, half_rows(k, 1 - zh))
             return 0
 
         lax.fori_loop(0, NX, ab_wait, 0)
-        for which in range(2):
-            hi, lo = split(ab[which])
-            abhi[which] = hi
-            ablo[which] = lo
         p = dot(abhi[0], abhi[1], NT)
         p += dot(ablo[0], abhi[1], NT)
         p += dot(abhi[0], ablo[1], NT)
@@ -368,6 +439,53 @@
         got(cs.at[3], cx_r.at[3])
         cseg[...] = mm3(cs[1], abhi[1], ablo[1], NT) + cs[3]
 
+    def x_sent():
+        @pl.when(outer)
+        def _():
+            for k in range(NX):
+                x_copy(k).wait_send()
+
+            @pl.when(x == 0)
+            def _():
+                cx_copy(0, 0, 1).wait_send()
+
+            @pl.when(x == 3)
+            def _():
+                cx_copy(3, 0, 2).wait_send()
+                cx_copy(3, 1, 1).wait_send()
+
+        @pl.when(root)
+        def _():
+            def ab_done(k, _):
+                abx_copy(k).wait_send()
+                abz_copy(k, w).wait_send()
+
+                @pl.when(k % 2 == 0)
+                def _():
+                    abz_copy(k, 1 - w).wait_send()
+
+                @pl.when(k % 2 == 1)
+                def _():
+                    abx_more(k).wait_send()
+
+                return 0
+
+            lax.fori_loop(0, NX, ab_done, 0)
+            cx_copy(1, 0, 3).wait_send()
+
+    block = jnp.where(x == xroot, 0, 4) + zi
+
+    def f0_copy():
+        return rcopy(f0_ref, f_in.at[block], f0_s, f0_r.at[block], did(seg, xroot, myend))
+
+    @pl.when(first & jnp.logical_not(root))
+    def _():
+        f0_copy().start()
+
+    @pl.when(first & root)
+    def _():
+        f_in[block] = f0_ref[...]
+
     m0 = jnp.concatenate([m0_ref[...], pad], axis=0)
     chained = root | (end & (x == 0))
 
@@ -380,18 +498,17 @@
         got(m_in, m_r)
 
     def m_copy(to, send):
-        return rcopy(m_out, m_in, m_s.at[send], m_r, did(seg + 1, to, end_z(1 - c, zh)))
-
-    def f_copy(q):
-        part = pl.ds(2 * q, 2)
-        return rcopy(f_out.at[part], f_in.at[part], f_s.at[q], f_r.at[q], did(seg + 1, x, end_z(1 - c, zh)))
+        return rcopy(m_out, m_in, m_s.at[send], m_r, did(seg + 1, to, end_z(way(seg + 1), zh)))
+
+    def f_copy(blk):
+        return rcopy(f_out.at[blk], f_in.at[blk], f_s.at[blk], f_r.at[blk], did(seg + 1, x, end_z(way(seg + 1), zh)))
 
     def owner(blk):
         return jnp.where(blk < 4, x, xouter), zh * 4 + blk % 4
 
     def fb_copy(blk):
         ox, oz = owner(blk)
-        return rcopy(f_out.at[blk], f_box, fb_s.at[blk], fb_r, did(seg, ox, oz))
+        return rcopy(f_out.at[blk], ends_ref.at[0], fb_s.at[blk], fb_r, did(seg, ox, oz))
 
     def ex_copy(to):
         return rcopy(e_out, e_x, ex_s, ex_r, did(seg, to, z))
@@ -413,41 +530,32 @@
             e_out[...] = mm3(e_x[...], wxhi[...], wxlo[...], NT) + cx[...]
             ex_copy(3).start()
 
-        def f_body(q, _):
-            for u in range(2):
-                blk = 2 * q + u
-
-                @pl.when(first & (blk != block))
-                def _():
-                    got(f_in.at[blk], f0_r.at[blk])
+        def f_body(blk, _):
+            @pl.when(first & (blk != block))
+            def _():
+                got(f_in.at[blk], f0_r.at[blk])
 
             @pl.when(jnp.logical_not(first))
             def _():
-                got(f_in.at[pl.ds(2 * q, 2)], f_r.at[q])
-
-            rows = jnp.concatenate([f_in[2 * q], f_in[2 * q + 1]], axis=0)
-            rows = mm3(rows, pfhi[...], pflo[...])
-            f_out[2 * q] = rows[:16]
-            f_out[2 * q + 1] = rows[16:]
+                got(f_in.at[blk], f_r.at[blk])
+
+            f_out[blk] = mm3(f_in[blk], pfhi[...], pflo[...])
 
             @pl.when(jnp.logical_not(last))
             def _():
-                f_copy(q).start()
-
-            for u in range(2):
-                blk = 2 * q + u
-
-                @pl.when(blk != block)
-                def _():
-                    fb_copy(blk).start()
-
-                @pl.when(blk == block)
-                def _():
-                    ends_ref[0] = f_out[blk]
+                f_copy(blk).start()
+
+            @pl.when(blk != block)
+            def _():
+                fb_copy(blk).start()
+
+            @pl.when(blk == block)
+            def _():
+                ends_ref[0] = f_out[blk]
 
             return 0
 
-        lax.fori_loop(0, 4, f_body, 0)
+        lax.fori_loop(0, 8, f_body, 0)
 
     @pl.when(end & (x == 0))
     def _():
@@ -502,83 +610,47 @@
 
     @pl.when(jnp.logical_not(root))
     def _():
-        got(f_box, fb_r)
-        ends_ref[0] = f_box[...]
-
-    def z_done(k, _):
-        z_copy(k).wait_send()
-        return 0
-
-    lax.fori_loop(0, NC, z_done, 0)
-
-    @pl.when(zi < 3)
-    def _():
-        c_next().wait_send()
-
-    @pl.when(zi == 3)
-    def _():
-        for half in range(2):
-            @pl.when(end_z(c, half) != z)
-            def _():
-                c_end(half).wait_send()
-
-    @pl.when(first & jnp.logical_not(root))
-    def _():
-        f0_copy().wait_send()
-
-    @pl.when(outer)
-    def _():
-        for k in range(NX):
-            x_copy(k).wait_send()
-
-        @pl.when(x == 0)
-        def _():
-            cx_copy(0, 0, 1).wait_send()
-
-        @pl.when(x == 3)
-        def _():
-            cx_copy(3, 0, 2).wait_send()
-            cx_copy(3, 1, 1).wait_send()
-
-    @pl.when(root)
-    def _():
-        def ab_done(k, _):
-            abx_copy(k).wait_send()
-            for which in range(2):
-                abz_copy(k, which).wait_send()
-            return 0
-
-        lax.fori_loop(0, NX, ab_done, 0)
-        cx_copy(1, 0, 3).wait_send()
-
-        @pl.when(jnp.logical_not(last))
-        def _():
-            m_copy(x, 0).wait_send()
-
-            @pl.when(x == 1)
-            def _():
-                m_copy(0, 1).wait_send()
-
-            for q in range(4):
-                f_copy(q).wait_send()
-
-        for blk in range(8):
-            @pl.when(blk != block)
-            def _():
-                fb_copy(blk).wait_send()
-
-    @pl.when(end & ((x == 0) | (x == 2)))
-    def _():
-        ex_copy(1).wait_send()
-
-    @pl.when(end & row)
-    def _():
-        for k in range(3):
-            e_copy(e_half, zh * 4 + k, k).wait_send()
-
-    @pl.when(jnp.logical_not(row) & (zi < 3))
-    def _():
-        e_copy(e_next, z + 1, 0).wait_send()
+        got(ends_ref.at[0], fb_r)
+
+    def rest_sent():
+        @pl.when(first & jnp.logical_not(root))
+        def _():
+            f0_copy().wait_send()
+
+        @pl.when(root)
+        def _():
+            @pl.when(jnp.logical_not(last))
+            def _():
+                m_copy(x, 0).wait_send()
+
+                @pl.when(x == 1)
+                def _():
+                    m_copy(0, 1).wait_send()
+
+                for blk in range(8):
+                    f_copy(blk).wait_send()
+
+            for blk in range(8):
+                @pl.when(blk != block)
+                def _():
+                    fb_copy(blk).wait_send()
+
+        @pl.when(end & ((x == 0) | (x == 2)))
+        def _():
+            ex_copy(1).wait_send()
+
+        @pl.when(end & row)
+        def _():
+            for k in range(3):
+                e_copy(e_half, zh * 4 + k, k).wait_send()
+
+        @pl.when(jnp.logical_not(row) & (zi < 3))
+        def _():
+            e_copy(e_next, z + 1, 0).wait_send()
+
+    z_sent()
+    x_sent()
+    rest_sent()
 
 
 def per_device(transition, obs_gain, observed, init_mean, init_factor):
@@ -588,10 +660,10 @@
     scratch = [
         f(D, D), f(2, D, D), b(D, D), b(D, D), f(2, PAD, D), f(PAD, D), f(2, PAD, D), f(PAD, D),
         b(2, D, D), b(2, D, D), f(D, D), b(D, D), b(D, D), f(HALF, D), f(2, D, D), b(2, D, D), b(2, D, D), b(D, D), b(D, D),
-        f(4, PAD, D), f(PAD, D), f(PAD, D), f(PAD, D), f(PAD, D), f(PAD, D), f(8, 16, D), f(8, 16, D), f(16, D), b(D, D), b(D, D),
+        f(4, PAD, D), f(PAD, D), f(PAD, D), f(PAD, D), f(PAD, D), f(PAD, D), f(8, 16, D), f(8, 16, D), b(D, D), b(D, D),
         f(PAD, D), f(PAD, D), f(PAD, D), f(PAD, D), f(PAD, D),
-        dma(NC), dma(2, NC), dma(), dma(), dma(2), dma(2), dma(NX), dma(NX), dma(NX), dma(NX), dma(2, NX), dma(2, NX),
-        dma(2), dma(4), dma(2), dma(), dma(), dma(8), dma(4), dma(4), dma(8), dma(), dma(3), dma(), dma(), dma(),
+        dma(NC), dma(2, NC), dma(), dma(), dma(2), dma(2), dma(NX), dma(NX), dma(NX), dma(NX), dma(NX), dma(NX), dma(2, NX), dma(2, NX),
+        dma(2), dma(4), dma(2), dma(), dma(), dma(8), dma(8), dma(8), dma(8), dma(), dma(3), dma(), dma(), dma(),
     ]
     return pl.pallas_call(
         kernel,

time: 103 us -> 94.2 us (0.915)
  the two profiles are of different devices: /device:TPU:123 before, /device:TPU:124 now
where the time goes in v1:
time: 94.2 us; the launch traced here: 94.1 us
  Pallas kernels  91.5 us (97%)
  local copies, waits for them, and re-layouts  1.95 us (2%)
    pallas_call x1, Pallas kernels, per_device(): pl.pallas_call(kernel, out_shape=(jax.ShapeDtypeStruct((2, 4, D), F32), j...  91.5 us
    unnamed x4, local copies, waits for them, and re-layouts  1.95 us

profile of v1, /device:TPU:124, one launch (start us, length us, event | category | flops | bytes accessed | tf_op | source)
XLA Modules:
  0.0 94.1 jit_solution(16123559997796421297)
XLA Ops:
  0.6 91.5 %filter_flow.1 = (f32[2,4,512]{2,1,0:T(4,128)}, f32[1,16,512]{2,1,0:T(8,128)}) custom-call(bf16[2,512,512]{2,1,0:T(8,128)(2,1)} %t_ref.1, bf16[2,512,512]{2,1,0:T(8,128)(2,1)} %g_ref.1, bf16[2,4,512]{2,1,0:T(4,128)(2,1)} %o_ref.1, f32[4,512]{1,0:T(4,128)} %m0_ref.1, f32[16,512]{1,0:T(8,128)} %f0_ref.1), custom_call_target="tpu_custom_call" | custom-call | tf_op jit(solution)/shard_map/filter_flow/pallas_call | solution.py:668
  92.1 0.0 copy-start
  92.1 1.3 %copy.9 = f32[2,4,512]{2,1,0:T(4,128)} copy(f32[2,4,512]{2,1,0:T(4,128)} %get-tuple-element.4) | data formatting | bytes 32768
  93.5 0.0 copy-done
  93.5 0.6 copy.10
Async XLA Ops:
  92.1 1.3 %copy-start = (f32[1,16,512]{2,1,0:T(8,128)S(1)}, f32[1,16,512]{2,1,0:T(8,128)}, u32[]{:S(2)}) copy-start(f32[1,16,512]{2,1,0:T(8,128)} %get-tuple-element.5) | copy-start | bytes 98308

commit v2 on v1

--- a/solution.py
+++ b/solution.py
@@ -15,6 +15,8 @@
 NC = D // ROWS
 NX = HALF // ROWS
 LAG = 4
+WIDE = 128
+NP = D // WIDE
 PAD = 8
 
 NN = (((1,), (0,)), ((), ()))
@@ -50,8 +52,8 @@
     t_ref, g_ref, o_ref, m0_ref, f0_ref, means_ref, ends_ref,
     zout, zin, whi, wlo, drv, cin, ch, csend,
     sphi, splo, px, wxhi, wxlo, xin, ab, abhi, ablo, pfhi, pflo,
-    cs, cx, cseg, cown, m_in, m_out, f_in, f_out, inhi, inlo, e_in, e_out, e_half, e_x, e_next,
-    zs, zr, cs_s, cs_r, ch_s, ch_r, xs, xr, abx_s, abx_r, abm_s, abm_r, abz_s, abz_r,
+    cs, cx, cseg, cown, m_in, m_out, f_in, f_out, inhi, inlo, e_in, e_out, e_half, e_x, pout,
+    ps, zs, zr, cs_s, cs_r, ch_s, ch_r, xs, xr, abx_s, abx_r, abm_s, abm_r, abz_s, abz_r,
     cx_s, cx_r, m_s, m_r, f0_s, f0_r, f_s, f_r, fb_s, fb_r, e_s, e_r, ex_s, ex_r,
 ):
     seg = lax.axis_index("seg")
@@ -180,6 +182,10 @@
     def _():
         put_map(dot(t_ref[1], t_ref[0], TT))
 
+        @pl.when(end)
+        def _():
+            pout[...] = dot(t_ref[0], t_ref[1])
+
     pad = jnp.zeros((PAD - 4, D), F32)
     for s in range(2):
         drv[s] = jnp.concatenate([dot(o_ref[s], g_ref[s]), pad], axis=0)
@@ -189,6 +195,19 @@
         cin[...] = jnp.zeros_like(cin)
 
     pl.semaphore_wait(barrier, greets)
+
+    block = jnp.where(x == xroot, 0, 4) + zi
+
+    def f0_copy():
+        return rcopy(f0_ref, f_in.at[block], f0_s, f0_r.at[block], did(seg, xroot, myend))
+
+    @pl.when(first & jnp.logical_not(root))
+    def _():
+        f0_copy().start()
+
+    @pl.when(first & root)
+    def _():
+        f_in[block] = f0_ref[...]
 
     def two_steps(m):
         m1 = mm2(m, t_ref[0]) + drv[0]
@@ -277,9 +296,37 @@
                 def _():
                     c_end(half).wait_send()
 
-    @pl.when(row & (pos > 0))
-    def _():
-        hi, lo = split(zin[0])
+    def wide(k):
+        return pl.ds(pl.multiple_of(k * WIDE, WIDE), WIDE)
+
+    def p_copy(k):
+        return rcopy(pout.at[wide(k)], zin.at[1, wide(k)], ps.at[k], zr.at[1, k], did(seg, x, z + 1))
+
+    def p_body(k, _):
+        got(zin.at[1, wide(k)], zr.at[1, k])
+
+        @pl.when(zi < 3)
+        def _():
+            pout[wide(k), :] = mm3(zin[1, wide(k), :], whi[...], wlo[...], NT)
+            p_copy(k).start()
+
+        return 0
+
+    def p_start(k, _):
+        p_copy(k).start()
+        return 0
+
+    def p_done(k, _):
+        p_copy(k).wait_send()
+        return 0
+
+    @pl.when(jnp.logical_not(row | end))
+    def _():
+        lax.fori_loop(0, NP, p_body, 0)
+
+    @pl.when(zi > 0)
+    def _():
+        hi, lo = split(zin[jnp.where(row, 0, 1)])
         inhi[...] = hi
         inlo[...] = lo
 
@@ -376,6 +423,10 @@
             cown[...] = mm3(cs[2], wxhi[...], wxlo[...], NT) + cx[...]
             cx_copy(3, 0, 2).start()
             cx_copy(3, 1, 1).start()
+
+    @pl.when(end & jnp.logical_not(row))
+    def _():
+        lax.fori_loop(0, NP, p_start, 0)
 
     @pl.when(root)
     def _():
@@ -473,19 +524,6 @@
             lax.fori_loop(0, NX, ab_done, 0)
             cx_copy(1, 0, 3).wait_send()
 
-    block = jnp.where(x == xroot, 0, 4) + zi
-
-    def f0_copy():
-        return rcopy(f0_ref, f_in.at[block], f0_s, f0_r.at[block], did(seg, xroot, myend))
-
-    @pl.when(first & jnp.logical_not(root))
-    def _():
-        f0_copy().start()
-
-    @pl.when(first & root)
-    def _():
-        f_in[block] = f0_ref[...]
-
     m0 = jnp.concatenate([m0_ref[...], pad], axis=0)
     chained = root | (end & (x == 0))
 
@@ -530,83 +568,87 @@
             e_out[...] = mm3(e_x[...], wxhi[...], wxlo[...], NT) + cx[...]
             ex_copy(3).start()
 
-        def f_body(blk, _):
-            @pl.when(first & (blk != block))
-            def _():
-                got(f_in.at[blk], f0_r.at[blk])
-
-            @pl.when(jnp.logical_not(first))
-            def _():
-                got(f_in.at[blk], f_r.at[blk])
-
-            f_out[blk] = mm3(f_in[blk], pfhi[...], pflo[...])
-
-            @pl.when(jnp.logical_not(last))
-            def _():
-                f_copy(blk).start()
-
-            @pl.when(blk != block)
-            def _():
-                fb_copy(blk).start()
-
-            @pl.when(blk == block)
-            def _():
-                ends_ref[0] = f_out[blk]
-
-            return 0
-
-        lax.fori_loop(0, 8, f_body, 0)
-
-    @pl.when(end & (x == 0))
-    def _():
-        e_out[...] = mm3(m_in[...], wxhi[...], wxlo[...]) + cx[...]
-        ex_copy(1).start()
-        e_x[...] = m_in[...]
-
-    @pl.when(end & ((x == 1) | (x == 3)))
-    def _():
-        got(e_x, ex_r)
-
-    @pl.when(end & (zh == 0))
-    def _():
-        e_half[...] = e_x[...]
-
-    for core, dims in ((0, NN), (1, NT)):
-        @pl.when(end & (zh == 1) & (c == core))
-        def _():
-            e_half[...] = mm3(e_x[...], sphi[1 - iv], splo[1 - iv], dims) + ch[0]
-
-    def e_copy(src, to, send):
-        return rcopy(src, e_in, e_s.at[send], e_r, did(seg, x, to))
-
-    @pl.when(end & row)
-    def _():
-        for k in range(3):
-            e_copy(e_half, zh * 4 + k, k).start()
-
-    @pl.when(jnp.logical_not(end))
-    def _():
-        got(e_in, e_r)
-        e_half[...] = e_in[...]
-
-    @pl.when(row & (pos > 0))
-    def _():
-        e_half_entry = mm3(e_half[...], inhi[...], inlo[...]) + cin[...]
-        m1, m2 = two_steps(e_half_entry)
+
+    def e_copy(k):
+        return rcopy(e_half, e_in, e_s.at[k], e_r, did(seg, x, zh * 4 + (zi + k + 1) % 4))
+
+    def go_down():
+        @pl.when(end & (x == 0))
+        def _():
+            e_out[...] = mm3(m_in[...], wxhi[...], wxlo[...]) + cx[...]
+            ex_copy(1).start()
+            e_x[...] = m_in[...]
+
+        @pl.when(end & ((x == 1) | (x == 3)))
+        def _():
+            got(e_x, ex_r)
+
+        @pl.when(end & (zh == 0))
+        def _():
+            e_half[...] = e_x[...]
+
+        for core, dims in ((0, NN), (1, NT)):
+            @pl.when(end & (zh == 1) & (c == core))
+            def _():
+                e_half[...] = mm3(e_x[...], sphi[1 - iv], splo[1 - iv], dims) + ch[0]
+
+        @pl.when(end)
+        def _():
+            for k in range(3):
+                e_copy(k).start()
+
+        @pl.when(jnp.logical_not(end))
+        def _():
+            got(e_in, e_r)
+            e_half[...] = e_in[...]
+
+        @pl.when(zi > 0)
+        def _():
+            e_in[...] = mm3(e_half[...], inhi[...], inlo[...]) + cin[...]
+
+        @pl.when(zi == 0)
+        def _():
+            e_in[...] = e_half[...]
+
+        m1, m2 = two_steps(e_in[...])
         means_ref[0] = m1[:4]
         means_ref[1] = m2[:4]
 
-    @pl.when(jnp.logical_not(row & (pos > 0)))
-    def _():
-        m1, m2 = two_steps(e_half[...])
-
-        @pl.when(jnp.logical_not(row) & (zi < 3))
-        def _():
-            e_next[...] = m2
-            e_copy(e_next, z + 1, 0).start()
-
-        means_ref[0] = m1[:4]
-        means_ref[1] = m2[:4]
+    def f_block(blk):
+        @pl.when(first & (blk != block))
+        def _():
+            got(f_in.at[blk], f0_r.at[blk])
+
+        @pl.when(jnp.logical_not(first))
+        def _():
+            got(f_in.at[blk], f_r.at[blk])
+
+        f_out[blk] = mm3(f_in[blk], pfhi[...], pflo[...])
+
+        @pl.when(jnp.logical_not(last))
+        def _():
+            f_copy(blk).start()
+
+        @pl.when(blk != block)
+        def _():
+            fb_copy(blk).start()
+
+        @pl.when(blk == block)
+        def _():
+            ends_ref[0] = f_out[blk]
+
+    down_turn = jnp.where(root, jnp.where(last, jnp.where(x == 2, 0, 6), 8), 0)
+
+    def chain_body(k, _):
+        pl.when(k == down_turn)(go_down)
+
+        @pl.when(root & (k < 8))
+        def _():
+            f_block(k)
+
+        return 0
+
+    lax.fori_loop(0, jnp.where(root, 9, 1), chain_body, 0)
 
     @pl.when(jnp.logical_not(root))
     def _():
@@ -639,14 +681,14 @@
         def _():
             ex_copy(1).wait_send()
 
-        @pl.when(end & row)
+        @pl.when(end)
         def _():
             for k in range(3):
-                e_copy(e_half, zh * 4 + k, k).wait_send()
+                e_copy(k).wait_send()
 
         @pl.when(jnp.logical_not(row) & (zi < 3))
         def _():
-            e_copy(e_next, z + 1, 0).wait_send()
+            lax.fori_loop(0, NP, p_done, 0)
 
     z_sent()
     x_sent()
@@ -661,8 +703,8 @@
         f(D, D), f(2, D, D), b(D, D), b(D, D), f(2, PAD, D), f(PAD, D), f(2, PAD, D), f(PAD, D),
         b(2, D, D), b(2, D, D), f(D, D), b(D, D), b(D, D), f(HALF, D), f(2, D, D), b(2, D, D), b(2, D, D), b(D, D), b(D, D),
         f(4, PAD, D), f(PAD, D), f(PAD, D), f(PAD, D), f(PAD, D), f(PAD, D), f(8, 16, D), f(8, 16, D), b(D, D), b(D, D),
-        f(PAD, D), f(PAD, D), f(PAD, D), f(PAD, D), f(PAD, D),
-        dma(NC), dma(2, NC), dma(), dma(), dma(2), dma(2), dma(NX), dma(NX), dma(NX), dma(NX), dma(NX), dma(NX), dma(2, NX), dma(2, NX),
+        f(PAD, D), f(PAD, D), f(PAD, D), f(PAD, D), f(D, D),
+        dma(NP), dma(NC), dma(2, NC), dma(), dma(), dma(2), dma(2), dma(NX), dma(NX), dma(NX), dma(NX), dma(NX), dma(NX), dma(2, NX), dma(2, NX),
         dma(2), dma(4), dma(2), dma(), dma(), dma(8), dma(8), dma(8), dma(8), dma(), dma(3), dma(), dma(), dma(),
     ]
     return pl.pallas_call(

time: 94.2 us -> 91.8 us (0.975)
  the two profiles are of different devices: /device:TPU:124 before, /device:TPU:31 now
where the time goes in v2:
time: 91.8 us; the launch traced here: 91.7 us
  Pallas kernels  89.1 us (97%)
  local copies, waits for them, and re-layouts  1.95 us (2%)
    pallas_call x1, Pallas kernels, per_device(): pl.pallas_call(kernel, out_shape=(jax.ShapeDtypeStruct((2, 4, D), F32), j...  89.1 us
    unnamed x4, local copies, waits for them, and re-layouts  1.95 us

profile of v2, /device:TPU:31, one launch (start us, length us, event | category | flops | bytes accessed | tf_op | source)
XLA Modules:
  0.0 91.7 jit_solution(16959391511932934625)
XLA Ops:
  0.6 89.1 %filter_flow.1 = (f32[2,4,512]{2,1,0:T(4,128)}, f32[1,16,512]{2,1,0:T(8,128)}) custom-call(bf16[2,512,512]{2,1,0:T(8,128)(2,1)} %t_ref.1, bf16[2,512,512]{2,1,0:T(8,128)(2,1)} %g_ref.1, bf16[2,4,512]{2,1,0:T(4,128)(2,1)} %o_ref.1, f32[4,512]{1,0:T(4,128)} %m0_ref.1, f32[16,512]{1,0:T(8,128)} %f0_ref.1), custom_call_target="tpu_custom_call" | custom-call | tf_op jit(solution)/shard_map/filter_flow/pallas_call | solution.py:710
  89.7 0.0 copy-start
  89.7 1.3 %copy.9 = f32[2,4,512]{2,1,0:T(4,128)} copy(f32[2,4,512]{2,1,0:T(4,128)} %get-tuple-element.4) | data formatting | bytes 32768
  91.1 0.0 copy-done
  91.1 0.6 copy.10
Async XLA Ops:
  89.7 1.3 %copy-start = (f32[1,16,512]{2,1,0:T(8,128)S(1)}, f32[1,16,512]{2,1,0:T(8,128)}, u32[]{:S(2)}) copy-start(f32[1,16,512]{2,1,0:T(8,128)} %get-tuple-element.5) | copy-start | bytes 98308

commit v3 on v2

--- a/solution.py
+++ b/solution.py
@@ -13,8 +13,9 @@
 HALF = D // 2
 ROWS = 32
 NC = D // ROWS
-NX = HALF // ROWS
-LAG = 4
+XROWS = 32
+NX = HALF // XROWS
+LAG = 6
 WIDE = 128
 NP = D // WIDE
 PAD = 8
@@ -334,10 +335,10 @@
     w = jnp.where(x == 1, 0, 1)
 
     def half_rows(k, half):
-        return pl.ds(pl.multiple_of(half * HALF + k * ROWS, ROWS), ROWS)
+        return pl.ds(pl.multiple_of(half * HALF + k * XROWS, XROWS), XROWS)
 
     def x_copy(k):
-        return rcopy(px.at[half_rows(k, zh)], xin.at[piece(k)], xs.at[k], xr.at[k], did(seg, xroot, z))
+        return rcopy(px.at[half_rows(k, zh)], xin.at[half_rows(k, 0)], xs.at[k], xr.at[k], did(seg, xroot, z))
 
     def abx_copy(k):
         return rcopy(
@@ -433,8 +434,8 @@
         def x_body(k, _):
             @pl.when(k < NX)
             def _():
-                got(xin.at[piece(k)], xr.at[k])
-                v = mm3(xin[piece(k), :], wxhi[...], wxlo[...])
+                got(xin.at[half_rows(k, 0)], xr.at[k])
+                v = mm3(xin[half_rows(k, 0), :], wxhi[...], wxlo[...])
                 mine = half_rows(k, zh)
                 ab[w, mine, :] = v
                 abx_copy(k).start()
@@ -562,17 +563,17 @@
             def _():
                 m_copy(0, 1).start()
 
-        @pl.when(x == 2)
+
+    def e_copy(k):
+        return rcopy(e_half, e_in, e_s.at[k], e_r, did(seg, x, zh * 4 + (zi + k + 1) % 4))
+
+    def go_down():
+        @pl.when(root & (x == 2))
         def _():
             e_x[...] = mm3(m_in[...], abhi[0], ablo[0]) + cs[1]
             e_out[...] = mm3(e_x[...], wxhi[...], wxlo[...], NT) + cx[...]
             ex_copy(3).start()
 
-
-    def e_copy(k):
-        return rcopy(e_half, e_in, e_s.at[k], e_r, did(seg, x, zh * 4 + (zi + k + 1) % 4))
-
-    def go_down():
         @pl.when(end & (x == 0))
         def _():
             e_out[...] = mm3(m_in[...], wxhi[...], wxlo[...]) + cx[...]
@@ -614,7 +615,18 @@
         means_ref[0] = m1[:4]
         means_ref[1] = m2[:4]
 
-    def f_block(blk):
+    def f_home(blk):
+        @pl.when(blk != block)
+        def _():
+            fb_copy(blk).start()
+
+        @pl.when(blk == block)
+        def _():
+            ends_ref[0] = f_out[blk]
+
+    def f_block(k):
+        blk = jnp.where(k < 4, 4, 0) + jnp.where(zh == 0, k % 4, 3 - k % 4)
+
         @pl.when(first & (blk != block))
         def _():
             got(f_in.at[blk], f0_r.at[blk])
@@ -629,13 +641,9 @@
         def _():
             f_copy(blk).start()
 
-        @pl.when(blk != block)
-        def _():
-            fb_copy(blk).start()
-
-        @pl.when(blk == block)
-        def _():
-            ends_ref[0] = f_out[blk]
+        @pl.when(last)
+        def _():
+            f_home(blk)
 
     down_turn = jnp.where(root, jnp.where(last, jnp.where(x == 2, 0, 6), 8), 0)
 
@@ -649,6 +657,11 @@
         return 0
 
     lax.fori_loop(0, jnp.where(root, 9, 1), chain_body, 0)
+
+    @pl.when(root & jnp.logical_not(last))
+    def _():
+        for blk in range(8):
+            f_home(blk)
 
     @pl.when(jnp.logical_not(root))
     def _():
@@ -707,7 +720,7 @@
         dma(NP), dma(NC), dma(2, NC), dma(), dma(), dma(2), dma(2), dma(NX), dma(NX), dma(NX), dma(NX), dma(NX), dma(NX), dma(2, NX), dma(2, NX),
         dma(2), dma(4), dma(2), dma(), dma(), dma(8), dma(8), dma(8), dma(8), dma(), dma(3), dma(), dma(), dma(),
     ]
-    return pl.pallas_call(
+    outs = pl.pallas_call(
         kernel,
         out_shape=(jax.ShapeDtypeStruct((2, 4, D), F32), jax.ShapeDtypeStruct((1, 16, D), F32)),
         in_specs=[vm] * 5,
@@ -719,6 +732,15 @@
         name="filter_flow",
     )(transition, obs_gain, observed, init_mean, init_factor)
 
+    def hand_on(a_ref, b_ref, a_out, b_out):
+        a_out[...] = a_ref[...]
+        b_out[...] = b_ref[...]
+
+    return pl.pallas_call(
+        hand_on, out_shape=tuple(jax.ShapeDtypeStruct(o.shape, o.dtype) for o in outs), in_specs=[vm] * 2, out_specs=(vm, vm),
+        name="hand_on",
+    )(*outs)
+
 
 def solution(mesh):
     placed = P(("seg", "tm"), None, None)

time: 91.8 us -> 88.7 us (0.966)
  the two profiles are of different devices: /device:TPU:31 before, /device:TPU:27 now
where the time goes in v3:
time: 88.7 us; the launch traced here: 88.5 us
  Pallas kernels  87.8 us (99%)
    pallas_call x1, Pallas kernels, per_device(): pl.pallas_call(kernel, out_shape=(jax.ShapeDtypeStruct((2, 4, D), F32), j...  86.4 us

profile of v3, /device:TPU:27, one launch (start us, length us, event | category | flops | bytes accessed | tf_op | source)
XLA Modules:
  0.0 88.5 jit_solution(7700683952076682904)
XLA Ops:
  0.6 86.4 %filter_flow.1 = (f32[2,4,512]{2,1,0:T(4,128)}, f32[1,16,512]{2,1,0:T(8,128)}) custom-call(bf16[2,512,512]{2,1,0:T(8,128)(2,1)} %t_ref.1, bf16[2,512,512]{2,1,0:T(8,128)(2,1)} %g_ref.1, bf16[2,4,512]{2,1,0:T(4,128)(2,1)} %o_ref.1, f32[4,512]{1,0:T(4,128)} %m0_ref.1, f32[16,512]{1,0:T(8,128)} %f0_ref.1), custom_call_target="tpu_custom_call" | custom-call | tf_op jit(solution)/shard_map/filter_flow/pallas_call | solution.py:723
  87.1 1.4 %hand_on.1 = (f32[2,4,512]{2,1,0:T(4,128)}, f32[1,16,512]{2,1,0:T(8,128)}) custom-call(f32[2,4,512]{2,1,0:T(4,128)} %get-tuple-element.4.a_ref, f32[1,16,512]{2,1,0:T(8,128)} %get-tuple-element.5.b_ref), custom_call_target="tpu_custom_call" | custom-call | tf_op jit(solution)/shard_map/hand_on/pallas_call | solution.py:739

commit v4 on v3

--- a/solution.py
+++ b/solution.py
@@ -54,14 +54,14 @@
     zout, zin, whi, wlo, drv, cin, ch, csend,
     sphi, splo, px, wxhi, wxlo, xin, ab, abhi, ablo, pfhi, pflo,
     cs, cx, cseg, cown, m_in, m_out, f_in, f_out, inhi, inlo, e_in, e_out, e_half, e_x, pout,
-    ps, zs, zr, cs_s, cs_r, ch_s, ch_r, xs, xr, abx_s, abx_r, abm_s, abm_r, abz_s, abz_r,
+    map_s, map_r, const_s, const_r, ps, zs, zr, cs_s, cs_r, ch_s, ch_r, xs, xr, abx_s, abx_r, abm_s, abm_r, abz_s, abz_r,
     cx_s, cx_r, m_s, m_r, f0_s, f0_r, f_s, f_r, fb_s, fb_r, e_s, e_r, ex_s, ex_r,
 ):
     seg = lax.axis_index("seg")
     tm = lax.axis_index("tm")
 
     def way(s):
-        return (s + s // 2) % 2
+        return jnp.where(s < 6, s + s // 2, s) % 2
 
     c = way(seg)
     x, z = tm // 8, tm % 8
@@ -85,6 +85,16 @@
 
     myend = end_z(c, zh)
 
+    def moved(s):
+        return (s == 5) | (s == 7)
+
+    def worker_z(s):
+        return end_z(jnp.where(moved(s), 0, way(s)), zh)
+
+    worker = inner & (z == worker_z(seg))
+    guest = worker & moved(seg)
+    host = root & moved(seg)
+
     def rcopy(src, dst, ssem, rsem, dev):
         return pltpu.make_async_remote_copy(
             src_ref=src, dst_ref=dst, send_sem=ssem, recv_sem=rsem, device_id=dev, device_id_type=MESH
@@ -135,33 +145,53 @@
     def _():
         greet(did(seg, xroot, myend))
 
-    @pl.when(root)
+        @pl.when(moved(seg))
+        def _():
+            greet(did(seg, xroot, worker_z(seg)))
+
+    @pl.when(root | guest)
     def _():
         for k in range(4):
             greet(did(seg, xouter, zh * 4 + k))
 
-        @pl.when(jnp.logical_not(last))
+    middle = inner & moved(seg) & ((pos == 1) | (pos == 2))
+
+    @pl.when(middle)
+    def _():
+        greet(did(seg, x, worker_z(seg)))
+
+    @pl.when(guest)
+    def _():
+        for k in (1, 2):
+            greet(did(seg, x, jnp.where(row, z + k, z - k)))
+
+    @pl.when(worker & jnp.logical_not(last))
+    def _():
+        greet(did(seg + 1, x, worker_z(seg + 1)))
+
+        @pl.when(moved(seg + 1))
         def _():
             greet(did(seg + 1, x, end_z(way(seg + 1), zh)))
 
-        @pl.when(jnp.logical_not(first))
-        def _():
-            greet(did(seg - 1, x, end_z(way(seg - 1), zh)))
-
-    @pl.when(root & (x == 1) & jnp.logical_not(last))
-    def _():
-        greet(did(seg + 1, 0, end_z(way(seg + 1), zh)))
+        @pl.when(x == 1)
+        def _():
+            greet(did(seg + 1, 0, end_z(way(seg + 1), zh)))
+
+    @pl.when((worker | host) & jnp.logical_not(first))
+    def _():
+        greet(did(seg - 1, x, worker_z(seg - 1)))
 
     @pl.when(end & (x == 0) & jnp.logical_not(first))
     def _():
-        greet(did(seg - 1, 1, end_z(way(seg - 1), zh)))
+        greet(did(seg - 1, 1, worker_z(seg - 1)))
 
     one = lambda p: jnp.where(p, 1, 0)
     greets = (
         one(pos < 3) + one((pos < 2) | end) + one((pos == 1) | (pos == 2)) + one((pos == 0) & jnp.logical_not(row))
         + one(end) * (3 + one(row) + jnp.where(x == 0, 1, jnp.where(x == 1, 3, 2))) + one(jnp.logical_not(inner))
-        + one(root) * (4 + one(jnp.logical_not(last)) + one(jnp.logical_not(first)))
-        + one(root & (x == 1) & jnp.logical_not(last)) + one(end & (x == 0) & jnp.logical_not(first))
+        + one(jnp.logical_not(inner) & moved(seg)) + 4 * one(root | guest) + one(middle) + 2 * one(guest)
+        + one(worker & jnp.logical_not(last)) * (1 + one(moved(seg + 1)) + one(x == 1))
+        + one((worker | host) & jnp.logical_not(first)) + one(end & (x == 0) & jnp.logical_not(first))
     )
 
     def put_map(m):
@@ -355,6 +385,12 @@
         return rcopy(
             ab.at[w, half_rows(k, 1 - zh)], ab.at[w, half_rows(k, 1 - zh)], abm_s.at[k], abm_r.at[k], did(seg, 3 - x, z)
         )
+
+    def map_copy(k):
+        return rcopy(px.at[wide(k)], zin.at[0, wide(k)], map_s.at[k], map_r.at[k], did(seg, x, worker_z(seg)))
+
+    def const_copy():
+        return rcopy(cseg, cseg, const_s, const_r, did(seg, x, worker_z(seg)))
 
     def ab_split(which, rows):
         abhi[which, rows, :], ablo[which, rows, :] = split(ab[which, rows, :])
@@ -480,6 +516,13 @@
         p = dot(abhi[0], abhi[1], NT)
         p += dot(ablo[0], abhi[1], NT)
         p += dot(abhi[0], ablo[1], NT)
+
+        @pl.when(host)
+        def _():
+            px[...] = p
+            for k in range(NP):
+                map_copy(k).start()
+
         hi, lo = split(p)
         pfhi[...] = hi
         pflo[...] = lo
@@ -491,6 +534,20 @@
         got(cs.at[3], cx_r.at[3])
         cseg[...] = mm3(cs[1], abhi[1], ablo[1], NT) + cs[3]
 
+        @pl.when(host)
+        def _():
+            const_copy().start()
+
+    @pl.when(guest)
+    def _():
+        def map_got(k, _):
+            got(zin.at[0, wide(k)], map_r.at[k])
+            pfhi[wide(k), :], pflo[wide(k), :] = split(zin[0, wide(k), :])
+            return 0
+
+        lax.fori_loop(0, NP, map_got, 0)
+        got(cseg, const_r)
+
     def x_sent():
         @pl.when(outer)
         def _():
@@ -526,7 +583,7 @@
             cx_copy(1, 0, 3).wait_send()
 
     m0 = jnp.concatenate([m0_ref[...], pad], axis=0)
-    chained = root | (end & (x == 0))
+    chained = root | guest | (end & (x == 0))
 
     @pl.when(chained & first)
     def _():
@@ -536,11 +593,13 @@
     def _():
         got(m_in, m_r)
 
-    def m_copy(to, send):
-        return rcopy(m_out, m_in, m_s.at[send], m_r, did(seg + 1, to, end_z(way(seg + 1), zh)))
+    def m_copy(send):
+        to = jnp.where(send == 1, 0, x)
+        at = jnp.where(send == 0, worker_z(seg + 1), end_z(way(seg + 1), zh))
+        return rcopy(m_out, m_in, m_s.at[send], m_r, did(seg + 1, to, at))
 
     def f_copy(blk):
-        return rcopy(f_out.at[blk], f_in.at[blk], f_s.at[blk], f_r.at[blk], did(seg + 1, x, end_z(way(seg + 1), zh)))
+        return rcopy(f_out.at[blk], f_in.at[blk], f_s.at[blk], f_r.at[blk], did(seg + 1, x, worker_z(seg + 1)))
 
     def owner(blk):
         return jnp.where(blk < 4, x, xouter), zh * 4 + blk % 4
@@ -552,16 +611,18 @@
     def ex_copy(to):
         return rcopy(e_out, e_x, ex_s, ex_r, did(seg, to, z))
 
-    @pl.when(root)
-    def _():
-        @pl.when(jnp.logical_not(last))
-        def _():
-            m_out[...] = mm3(m_in[...], pfhi[...], pflo[...]) + cseg[...]
-            m_copy(x, 0).start()
-
-            @pl.when(x == 1)
-            def _():
-                m_copy(0, 1).start()
+    @pl.when(worker & jnp.logical_not(last))
+    def _():
+        m_out[...] = mm3(m_in[...], pfhi[...], pflo[...]) + cseg[...]
+        m_copy(0).start()
+
+        @pl.when(x == 1)
+        def _():
+            m_copy(1).start()
+
+        @pl.when(moved(seg + 1))
+        def _():
+            m_copy(2).start()
 
 
     def e_copy(k):
@@ -645,25 +706,25 @@
         def _():
             f_home(blk)
 
-    down_turn = jnp.where(root, jnp.where(last, jnp.where(x == 2, 0, 6), 8), 0)
+    down_turn = jnp.where(worker, 8, 0)
 
     def chain_body(k, _):
         pl.when(k == down_turn)(go_down)
 
-        @pl.when(root & (k < 8))
+        @pl.when(worker & (k < 8))
         def _():
             f_block(k)
 
         return 0
 
-    lax.fori_loop(0, jnp.where(root, 9, 1), chain_body, 0)
-
-    @pl.when(root & jnp.logical_not(last))
+    lax.fori_loop(0, jnp.where(worker, 9, 1), chain_body, 0)
+
+    @pl.when(worker & jnp.logical_not(last))
     def _():
         for blk in range(8):
             f_home(blk)
 
-    @pl.when(jnp.logical_not(root))
+    @pl.when(jnp.logical_not(worker))
     def _():
         got(ends_ref.at[0], fb_r)
 
@@ -672,15 +733,19 @@
         def _():
             f0_copy().wait_send()
 
-        @pl.when(root)
+        @pl.when(worker)
         def _():
             @pl.when(jnp.logical_not(last))
             def _():
-                m_copy(x, 0).wait_send()
+                m_copy(0).wait_send()
 
                 @pl.when(x == 1)
                 def _():
-                    m_copy(0, 1).wait_send()
+                    m_copy(1).wait_send()
+
+                @pl.when(moved(seg + 1))
+                def _():
+                    m_copy(2).wait_send()
 
                 for blk in range(8):
                     f_copy(blk).wait_send()
@@ -702,6 +767,12 @@
         @pl.when(jnp.logical_not(row) & (zi < 3))
         def _():
             lax.fori_loop(0, NP, p_done, 0)
+
+        @pl.when(host)
+        def _():
+            const_copy().wait_send()
+            for k in range(NP):
+                map_copy(k).wait_send()
 
     z_sent()
     x_sent()
@@ -717,8 +788,8 @@
         b(2, D, D), b(2, D, D), f(D, D), b(D, D), b(D, D), f(HALF, D), f(2, D, D), b(2, D, D), b(2, D, D), b(D, D), b(D, D),
         f(4, PAD, D), f(PAD, D), f(PAD, D), f(PAD, D), f(PAD, D), f(PAD, D), f(8, 16, D), f(8, 16, D), b(D, D), b(D, D),
         f(PAD, D), f(PAD, D), f(PAD, D), f(PAD, D), f(D, D),
-        dma(NP), dma(NC), dma(2, NC), dma(), dma(), dma(2), dma(2), dma(NX), dma(NX), dma(NX), dma(NX), dma(NX), dma(NX), dma(2, NX), dma(2, NX),
-        dma(2), dma(4), dma(2), dma(), dma(), dma(8), dma(8), dma(8), dma(8), dma(), dma(3), dma(), dma(), dma(),
+        dma(NP), dma(NP), dma(), dma(), dma(NP), dma(NC), dma(2, NC), dma(), dma(), dma(2), dma(2), dma(NX), dma(NX), dma(NX), dma(NX), dma(NX), dma(NX), dma(2, NX), dma(2, NX),
+        dma(2), dma(4), dma(3), dma(), dma(), dma(8), dma(8), dma(8), dma(8), dma(), dma(3), dma(), dma(), dma(),
     ]
     outs = pl.pallas_call(
         kernel,

time: 88.7 us -> 90.8 us (1.024)
  the two profiles are of different devices: /device:TPU:27 before, /device:TPU:24 now
where the time goes in v4:
time: 90.8 us; the launch traced here: 90.6 us
  Pallas kernels  90 us (99%)
    pallas_call x1, Pallas kernels, per_device(): pl.pallas_call(kernel, out_shape=(jax.ShapeDtypeStruct((2, 4, D), F32), j...  88.6 us

profile of v4, /device:TPU:24, one launch (start us, length us, event | category | flops | bytes accessed | tf_op | source)
XLA Modules:
  0.0 90.6 jit_solution(3432324374438271572)
XLA Ops:
  0.6 88.6 %filter_flow.1 = (f32[2,4,512]{2,1,0:T(4,128)}, f32[1,16,512]{2,1,0:T(8,128)}) custom-call(bf16[2,512,512]{2,1,0:T(8,128)(2,1)} %t_ref.1, bf16[2,512,512]{2,1,0:T(8,128)(2,1)} %g_ref.1, bf16[2,4,512]{2,1,0:T(4,128)(2,1)} %o_ref.1, f32[4,512]{1,0:T(4,128)} %m0_ref.1, f32[16,512]{1,0:T(8,128)} %f0_ref.1), custom_call_target="tpu_custom_call" | custom-call | tf_op jit(solution)/shard_map/filter_flow/pallas_call | solution.py:794
  89.2 1.4 %hand_on.1 = (f32[2,4,512]{2,1,0:T(4,128)}, f32[1,16,512]{2,1,0:T(8,128)}) custom-call(f32[2,4,512]{2,1,0:T(4,128)} %get-tuple-element.4.a_ref, f32[1,16,512]{2,1,0:T(8,128)} %get-tuple-element.5.b_ref), custom_call_target="tpu_custom_call" | custom-call | tf_op jit(solution)/shard_map/hand_on/pallas_call | solution.py:810

commit v5 on v4

--- a/solution.py
+++ b/solution.py
@@ -351,15 +351,18 @@
         p_copy(k).wait_send()
         return 0
 
-    @pl.when(jnp.logical_not(row | end))
-    def _():
-        lax.fori_loop(0, NP, p_body, 0)
-
-    @pl.when(zi > 0)
-    def _():
-        hi, lo = split(zin[jnp.where(row, 0, 1)])
-        inhi[...] = hi
-        inlo[...] = lo
+    def prefix():
+        @pl.when(jnp.logical_not(row | end))
+        def _():
+            lax.fori_loop(0, NP, p_body, 0)
+
+        @pl.when(zi > 0)
+        def _():
+            hi, lo = split(zin[jnp.where(row, 0, 1)])
+            inhi[...] = hi
+            inlo[...] = lo
+
+    pl.when(jnp.logical_not(guest))(prefix)
 
     iv = jnp.where(x < 2, 1, 0)
     w = jnp.where(x == 1, 0, 1)
@@ -629,6 +632,8 @@
         return rcopy(e_half, e_in, e_s.at[k], e_r, did(seg, x, zh * 4 + (zi + k + 1) % 4))
 
     def go_down():
+        pl.when(guest)(prefix)
+
         @pl.when(root & (x == 2))
         def _():
             e_x[...] = mm3(m_in[...], abhi[0], ablo[0]) + cs[1]

time: 90.8 us -> 87.3 us (0.961)
  Pallas kernels: 90 us -> 85.9 us
    pallas_call x1, Pallas kernels: 88.6 us -> 84.5 us  [per_device(): pl.pallas_call(kernel, out_shape=(jax.ShapeDtypeStruct((2, 4, D), F32), j...]
where the time goes in v5:
time: 87.3 us; the launch traced here: 86.6 us
  Pallas kernels  85.9 us (98%)
    pallas_call x1, Pallas kernels, per_device(): pl.pallas_call(kernel, out_shape=(jax.ShapeDtypeStruct((2, 4, D), F32), j...  84.5 us

profile of v5, /device:TPU:24, one launch (start us, length us, event | category | flops | bytes accessed | tf_op | source)
XLA Modules:
  0.0 86.6 jit_solution(7088238400753719658)
XLA Ops:
  0.6 84.5 %filter_flow.1 = (f32[2,4,512]{2,1,0:T(4,128)}, f32[1,16,512]{2,1,0:T(8,128)}) custom-call(bf16[2,512,512]{2,1,0:T(8,128)(2,1)} %t_ref.1, bf16[2,512,512]{2,1,0:T(8,128)(2,1)} %g_ref.1, bf16[2,4,512]{2,1,0:T(4,128)(2,1)} %o_ref.1, f32[4,512]{1,0:T(4,128)} %m0_ref.1, f32[16,512]{1,0:T(8,128)} %f0_ref.1), custom_call_target="tpu_custom_call" | custom-call | tf_op jit(solution)/shard_map/filter_flow/pallas_call | solution.py:799
  85.2 1.4 %hand_on.1 = (f32[2,4,512]{2,1,0:T(4,128)}, f32[1,16,512]{2,1,0:T(8,128)}) custom-call(f32[2,4,512]{2,1,0:T(4,128)} %get-tuple-element.4.a_ref, f32[1,16,512]{2,1,0:T(8,128)} %get-tuple-element.5.b_ref), custom_call_target="tpu_custom_call" | custom-call | tf_op jit(solution)/shard_map/hand_on/pallas_call | solution.py:815

commit v6 on v5

--- a/solution.py
+++ b/solution.py
@@ -713,21 +713,22 @@
 
     down_turn = jnp.where(worker, 8, 0)
 
-    def chain_body(k, _):
-        pl.when(k == down_turn)(go_down)
-
-        @pl.when(worker & (k < 8))
-        def _():
-            f_block(k)
-
-        return 0
-
-    lax.fori_loop(0, jnp.where(worker, 9, 1), chain_body, 0)
-
-    @pl.when(worker & jnp.logical_not(last))
-    def _():
+    def all_home():
         for blk in range(8):
             f_home(blk)
+
+    def chain_body(k, _):
+        pl.when((k == 8) & worker & jnp.logical_not(last))(all_home)
+        pl.when(k == down_turn)(go_down)
+
+        @pl.when(worker & (k < 8))
+        def _():
+            f_block(k)
+
+        return 0
+
+    lax.fori_loop(0, jnp.where(worker, 9, 1), chain_body, 0)
+
 
     @pl.when(jnp.logical_not(worker))
     def _():

time: 87.3 us -> 86.6 us (level)
  no operation moved by 1% of the time
where the time goes in v6:
time: 86.6 us; the launch traced here: 86 us
  Pallas kernels  85.4 us (99%)
    pallas_call x1, Pallas kernels, per_device(): pl.pallas_call(kernel, out_shape=(jax.ShapeDtypeStruct((2, 4, D), F32), j...  84 us

profile of v6, /device:TPU:24, one launch (start us, length us, event | category | flops | bytes accessed | tf_op | source)
XLA Modules:
  0.0 86.0 jit_solution(16692477213307795243)
XLA Ops:
  0.6 84.0 %filter_flow.1 = (f32[2,4,512]{2,1,0:T(4,128)}, f32[1,16,512]{2,1,0:T(8,128)}) custom-call(bf16[2,512,512]{2,1,0:T(8,128)(2,1)} %t_ref.1, bf16[2,512,512]{2,1,0:T(8,128)(2,1)} %g_ref.1, bf16[2,4,512]{2,1,0:T(4,128)(2,1)} %o_ref.1, f32[4,512]{1,0:T(4,128)} %m0_ref.1, f32[16,512]{1,0:T(8,128)} %f0_ref.1), custom_call_target="tpu_custom_call" | custom-call | tf_op jit(solution)/shard_map/filter_flow/pallas_call | solution.py:800
  84.7 1.4 %hand_on.1 = (f32[2,4,512]{2,1,0:T(4,128)}, f32[1,16,512]{2,1,0:T(8,128)}) custom-call(f32[2,4,512]{2,1,0:T(4,128)} %get-tuple-element.4.a_ref, f32[1,16,512]{2,1,0:T(8,128)} %get-tuple-element.5.b_ref), custom_call_target="tpu_custom_call" | custom-call | tf_op jit(solution)/shard_map/hand_on/pallas_call | solution.py:816

commit v7 on v6

--- a/solution.py
+++ b/solution.py
@@ -15,7 +15,7 @@
 NC = D // ROWS
 XROWS = 32
 NX = HALF // XROWS
-LAG = 6
+LAG = 8
 WIDE = 128
 NP = D // WIDE
 PAD = 8

time: 86.6 us -> 86.6 us (level)
  no operation moved by 1% of the time
where the time goes in v7:
time: 86.6 us; the launch traced here: 86 us
  Pallas kernels  85.4 us (99%)
    pallas_call x1, Pallas kernels, per_device(): pl.pallas_call(kernel, out_shape=(jax.ShapeDtypeStruct((2, 4, D), F32), j...  84 us

profile of v7, /device:TPU:24, one launch (start us, length us, event | category | flops | bytes accessed | tf_op | source)
XLA Modules:
  0.0 86.0 jit_solution(12217471487668264684)
XLA Ops:
  0.6 84.0 %filter_flow.1 = (f32[2,4,512]{2,1,0:T(4,128)}, f32[1,16,512]{2,1,0:T(8,128)}) custom-call(bf16[2,512,512]{2,1,0:T(8,128)(2,1)} %t_ref.1, bf16[2,512,512]{2,1,0:T(8,128)(2,1)} %g_ref.1, bf16[2,4,512]{2,1,0:T(4,128)(2,1)} %o_ref.1, f32[4,512]{1,0:T(4,128)} %m0_ref.1, f32[16,512]{1,0:T(8,128)} %f0_ref.1), custom_call_target="tpu_custom_call" | custom-call | tf_op jit(solution)/shard_map/filter_flow/pallas_call | solution.py:800
  84.7 1.4 %hand_on.1 = (f32[2,4,512]{2,1,0:T(4,128)}, f32[1,16,512]{2,1,0:T(8,128)}) custom-call(f32[2,4,512]{2,1,0:T(4,128)} %get-tuple-element.4.a_ref, f32[1,16,512]{2,1,0:T(8,128)} %get-tuple-element.5.b_ref), custom_call_target="tpu_custom_call" | custom-call | tf_op jit(solution)/shard_map/hand_on/pallas_call | solution.py:816
